TPU v7x, 32 devices: a whole 2x2x4 slice. The times are simulated.
32 devices in a mesh: parts: 2 (over y), band: 4 (over z), feat: 2 (over x), rep: 2 (over core).
Axes of the slice: x: 2, y: 2, z: 4, core: 2. Of those that a mesh axis runs over, the one named last changes fastest.
Arguments:
- grid_in: bfloat16 [8192, 520], P(('parts', 'band', 'feat', 'rep')), parts along dimension 0, may hold values from -6 to 6
- target: bfloat16 [8192, 520], P(('parts', 'band', 'feat', 'rep')), parts along dimension 0, may hold values from -6 to 6
- mesh_in: bfloat16 [4096, 512], P(('parts', 'band', 'feat', 'rep')), parts along dimension 0, may hold values from -6 to 6
- embed_weight: bfloat16 [520, 512], P(None, 'feat'), may hold values from -0.25 to 0.25
- encode_project: bfloat16 [512, 512], P(None, 'feat'), may hold values from -0.25 to 0.25
- encode_attr_weight: bfloat16 [4, 512], replicated, may hold values from -3 to 3
- encode_edge_weight: bfloat16 [512, 512], P(None, 'feat'), may hold values from -0.25 to 0.25
- node_weight: bfloat16 [512, 512], P(None, 'feat'), may hold values from -0.25 to 0.25
- node_gain: bfloat16 [512], replicated, may hold values from 0.099609375 to 1.8984375
- decode_project: bfloat16 [512, 512], P(None, 'feat'), may hold values from -0.25 to 0.25
- decode_attr_weight: bfloat16 [4, 512], replicated, may hold values from -3 to 3
- decode_edge_weight: bfloat16 [512, 512], P(None, 'feat'), may hold values from -0.25 to 0.25
- out_weight: bfloat16 [512, 520], replicated, may hold values from -0.25 to 0.25
- encode_senders: int32 [32, 4, 32], P(('parts', 'band', 'feat', 'rep')), parts along dimension 0, may hold values from 0 to 255, as said below
- encode_receivers: int32 [32, 4, 32], P(('parts', 'band', 'feat', 'rep')), parts along dimension 0, may hold values from -1 to 127, as said below
- encode_features: bfloat16 [32, 4, 128], P(('parts', 'band', 'feat', 'rep')), parts along dimension 0, may hold values from -6 to 6
- decode_senders: int32 [32, 4, 64], P(('parts', 'band', 'feat', 'rep')), parts along dimension 0, may hold values from 0 to 127, as said below
- decode_receivers: int32 [32, 4, 64], P(('parts', 'band', 'feat', 'rep')), parts along dimension 0, may hold values from -1 to 255, as said below
- decode_features: bfloat16 [32, 4, 256], P(('parts', 'band', 'feat', 'rep')), parts along dimension 0, may hold values from -6 to 6
Outputs:
- predicted: bfloat16 [8192, 520], P(('parts', 'band', 'feat', 'rep')), parts along dimension 0
- edge_gradient: float32 [1024, 512], P('parts', 'feat'), parts along dimension 0
There are 2 independent parts, one for each index of `parts`. A program takes and returns all parts, laid end to end along the dimension named above; an argument that names none is the same for every part. Nothing has to cross between parts.
Inputs may be any that keep to these rules, and one draw needn't show every extreme that they name: encode_senders[k, p, c] is a row within the 256 grid points of slab k. encode_receivers[j, b, c] is a row within the 128 mesh nodes of slab j, or -1 for an empty slot. The used slots of a block come first. A block from band b to partition p is empty when p and b differ by more than 2; it uses 1 to 16 slots when they differ by at most 1, and 1 to 8 when they differ by 2. For one partition, drawn from the seed, every block bound to it from a band within 2 of it is full (32 slots). decode_senders[j, b, c] is a row within the 128 mesh nodes of slab j. decode_receivers[k, p, c] is a row within the 256 grid points of slab k, or -1 for an empty slot. The used slots of a block come first. A block from partition p to band b is empty when p and b differ by more than 2; it uses 1 to 32 slots when they differ by at most 1, and 1 to 16 when they differ by 2. For one band, drawn from the seed, every block bound to it from a partition within 2 of it is full (64 slots).
All inputs are finite; a program needn't handle non-finite values.
Results may differ from a plain program's by a relative error of at most 0.0075.
Values may be sent and summed in bfloat16 or wider, within the bound.
A program may use at most 64 MiB of HBM per device.

v0:
```python
import math

import jax
import jax.numpy as jnp
from jax import lax
from jax.sharding import PartitionSpec as P

eps_norm = 1e-05


def project(activation, shard):
    return jnp.dot(
        activation,
        lax.all_gather(shard, "feat", axis=1, tiled=True),
        preferred_element_type=jnp.float32,
    )


def pick_rows(node_table, index_block):
    flat_index = index_block.reshape(-1)
    onehot = (
        flat_index[:, None] == jnp.arange(node_table.shape[0], dtype=jnp.int32)[None, :]
    ).astype(jnp.bfloat16)
    return jnp.dot(onehot, node_table, preferred_element_type=jnp.float32)


def collect_rows(values, index_block, row_count):
    flat_index = index_block.reshape(-1)
    onehot = (jnp.arange(row_count, dtype=jnp.int32)[:, None] == flat_index[None, :]).astype(
        jnp.bfloat16
    )
    return jnp.dot(onehot, values, preferred_element_type=jnp.float32)


def edge_inputs(node_table, index_block, features, attr_weight):
    attr_term = lax.dot_general(
        features, attr_weight, (((0,), (0,)), ((), ())), preferred_element_type=jnp.float32
    )
    return jax.nn.silu(pick_rows(node_table, index_block) + attr_term).astype(jnp.bfloat16)


def predict(grid_latent, incoming, target, out_weight, grid_total):
    decoded = (grid_latent.astype(jnp.float32) + incoming).astype(jnp.bfloat16)
    predicted = jnp.dot(decoded, out_weight, preferred_element_type=jnp.float32).astype(
        jnp.bfloat16
    )
    error = (
        (predicted.astype(jnp.float32) - target.astype(jnp.float32)) / math.sqrt(grid_total)
    ).astype(jnp.bfloat16)
    grid_cotangent = lax.dot_general(
        error, out_weight, (((1,), (1,)), ((), ())), preferred_element_type=jnp.float32
    ).astype(jnp.bfloat16)
    return (predicted, grid_cotangent)


def local(
    grid_in,
    target,
    mesh_in,
    embed_weight,
    encode_project,
    encode_attr_weight,
    encode_edge_weight,
    node_weight,
    node_gain,
    decode_project,
    decode_attr_weight,
    decode_edge_weight,
    out_weight,
    encode_senders,
    encode_receivers,
    encode_features,
    decode_senders,
    decode_receivers,
    decode_features,
):
    grid_rows = grid_in.shape[0]
    mesh_rows = mesh_in.shape[0]
    width = mesh_in.shape[1]
    peers = encode_senders.shape[1]
    grid_total = grid_rows * lax.axis_size("band") * lax.axis_size("feat") * lax.axis_size("rep")
    grid_latent = jax.nn.silu(project(grid_in, embed_weight)).astype(jnp.bfloat16)
    grid_project = project(grid_latent, encode_project).astype(jnp.bfloat16)
    encode_act = edge_inputs(
        grid_project, encode_senders[0], encode_features[0], encode_attr_weight
    )
    encode_message = project(encode_act, encode_edge_weight).astype(jnp.bfloat16)
    arrived = lax.all_to_all(
        encode_message.reshape(peers, -1, width), "band", split_axis=0, concat_axis=0, tiled=True
    )
    aggregated = collect_rows(arrived.reshape(-1, width), encode_receivers[0], mesh_rows).astype(
        jnp.bfloat16
    )
    update = mesh_in.astype(jnp.float32) + project(aggregated, node_weight)
    centre = jnp.mean(update, axis=-1, keepdims=True)
    centered = update - centre
    spread = jnp.mean(centered * centered, axis=-1, keepdims=True)
    mesh_latent = (node_gain.astype(jnp.float32) * centered * lax.rsqrt(spread + eps_norm)).astype(
        jnp.bfloat16
    )
    mesh_project = project(mesh_latent, decode_project).astype(jnp.bfloat16)
    decode_act = edge_inputs(
        mesh_project, decode_senders[0], decode_features[0], decode_attr_weight
    )
    decode_message = project(decode_act, decode_edge_weight).astype(jnp.bfloat16)
    landed = lax.all_to_all(
        decode_message.reshape(peers, -1, width), "band", split_axis=0, concat_axis=0, tiled=True
    )
    incoming = collect_rows(landed.reshape(-1, width), decode_receivers[0], grid_rows)
    predicted, grid_cotangent = predict(grid_latent, incoming, target, out_weight, grid_total)
    slot_cotangent = pick_rows(grid_cotangent, decode_receivers[0]).astype(jnp.bfloat16)
    returned = lax.all_to_all(
        slot_cotangent.reshape(peers, -1, width), "band", split_axis=0, concat_axis=0, tiled=True
    )
    term = lax.dot_general(
        decode_act,
        returned.reshape(-1, width),
        (((0,), (0,)), ((), ())),
        preferred_element_type=jnp.float32,
    )
    columns = width // lax.axis_size("feat")
    total = lax.psum(term, ("band", "feat", "rep"))
    edge_gradient = lax.dynamic_slice_in_dim(total, lax.axis_index("feat") * columns, columns, 1)
    return (predicted, edge_gradient)


def solution(mesh):
    return jax.shard_map(
        local,
        mesh=mesh,
        in_specs=(
            P(("parts", "band", "feat", "rep"), None),
            P(("parts", "band", "feat", "rep"), None),
            P(("parts", "band", "feat", "rep"), None),
            P(None, "feat"),
            P(None, "feat"),
            P(),
            P(None, "feat"),
            P(None, "feat"),
            P(),
            P(None, "feat"),
            P(),
            P(None, "feat"),
            P(),
            P(("parts", "band", "feat", "rep"), None, None),
            P(("parts", "band", "feat", "rep"), None, None),
            P(("parts", "band", "feat", "rep"), None, None),
            P(("parts", "band", "feat", "rep"), None, None),
            P(("parts", "band", "feat", "rep"), None, None),
            P(("parts", "band", "feat", "rep"), None, None),
        ),
        out_specs=(P(("parts", "band", "feat", "rep"), None), P("parts", "feat")),
        check_vma=False,
    )
```

profile of v0, /device:TPU:0, one launch (start us, length us, event | category | flops | bytes accessed | tf_op | source)
XLA Modules:
  0.0 196.4 jit_solution(10317813720431663049)
XLA Ops:
  7.2 10.4 %all_gather.18 = bf16[520,512]{1,0:T(8,128)(2,1)S(1)} all-gather(bf16[520,256]{1,0:T(8,128)(2,1)} %param.22), channel_id=1, replica_groups=mesh['parts'=2,'band'=4,'feat'=2,'rep'=2] {'feat'}, dimensions={1}, use_global_device_ids=true | all-gather | bytes 798720 | tf_op jit(solution)/shard_map/all_gather | solution.py:14
  17.6 8.3 %all_gather.19 = bf16[512,512]{1,0:T(8,128)(2,1)S(1)} all-gather(bf16[512,256]{1,0:T(8,128)(2,1)S(1)} %copy-done.2), channel_id=1, replica_groups=mesh['parts'=2,'band'=4,'feat'=2,'rep'=2] {'feat'}, dimensions={1}, use_global_device_ids=true | all-gather | bytes 786432 | tf_op jit(solution)/shard_map/all_gather | solution.py:14
  26.0 7.4 %all_gather.20 = bf16[512,512]{1,0:T(8,128)(2,1)S(1)} all-gather(bf16[512,256]{1,0:T(8,128)(2,1)S(1)} %copy-done.3), channel_id=1, replica_groups=mesh['parts'=2,'band'=4,'feat'=2,'rep'=2] {'feat'}, dimensions={1}, use_global_device_ids=true | all-gather | bytes 786432 | tf_op jit(solution)/shard_map/all_gather | solution.py:14
  33.4 0.4 fusion.26
  34.3 0.5 multiply_convert_fusion.6
  34.8 0.9 convolution_convert_fusion.6
  35.7 4.7 %all-to-all-start = ((bf16[4,32,512]{2,1,0:T(8,128)(2,1)}), bf16[4,32,512]{2,1,0:T(8,128)(2,1)S(1)}, u32[]{:S(2)}, u32[]{:S(2)}) async-start(bf16[4,32,512]{2,1,0:T(8,128)(2,1)} %bitcast.1), calls=%async_computation | async-start | bytes 262144 | tf_op jit(solution)/shard_map/all_to_all | solution.py:88
  40.4 8.2 %all_gather.21 = bf16[512,512]{1,0:T(8,128)(2,1)S(1)} all-gather(bf16[512,256]{1,0:T(8,128)(2,1)S(1)} %copy-done.4), channel_id=1, replica_groups=mesh['parts'=2,'band'=4,'feat'=2,'rep'=2] {'feat'}, dimensions={1}, use_global_device_ids=true | all-gather | bytes 786432 | tf_op jit(solution)/shard_map/all_gather | solution.py:14
  48.7 7.9 %all_gather.22 = bf16[512,512]{1,0:T(8,128)(2,1)S(1)} all-gather(bf16[512,256]{1,0:T(8,128)(2,1)S(1)} %copy-done.5), channel_id=1, replica_groups=mesh['parts'=2,'band'=4,'feat'=2,'rep'=2] {'feat'}, dimensions={1}, use_global_device_ids=true | all-gather | bytes 786432 | tf_op jit(solution)/shard_map/all_gather | solution.py:14
  56.6 0.6 copy-done.14
  57.2 0.7 copy-done.11
  58.0 7.2 %all_gather.23 = bf16[512,512]{1,0:T(8,128)(2,1)S(1)} all-gather(bf16[512,256]{1,0:T(8,128)(2,1)S(1)} %copy-done.6), channel_id=1, replica_groups=mesh['parts'=2,'band'=4,'feat'=2,'rep'=2] {'feat'}, dimensions={1}, use_global_device_ids=true | all-gather | bytes 786432 | tf_op jit(solution)/shard_map/all_gather | solution.py:14
  65.2 0.4 fusion.25
  65.8 0.5 fusion.3
  66.9 1.0 convolution_convert_fusion.3
  67.9 5.2 %all-to-all-start.1 = ((bf16[4,64,512]{2,1,0:T(8,128)(2,1)}), bf16[4,64,512]{2,1,0:T(8,128)(2,1)S(1)}, u32[]{:S(2)}, u32[]{:S(2)}) async-start(bf16[4,64,512]{2,1,0:T(8,128)(2,1)} %bitcast.4), calls=%async_computation.1 | async-start | bytes 524288 | tf_op jit(solution)/shard_map/all_to_all | solution.py:106
  73.2 6.8 %all-to-all-done.1 = bf16[4,64,512]{2,1,0:T(8,128)(2,1)S(1)} async-done(((bf16[4,64,512]{2,1,0:T(8,128)(2,1)}), bf16[4,64,512]{2,1,0:T(8,128)(2,1)S(1)}, u32[]{:S(2)}, u32[]{:S(2)}) %all-to-all-start.1) | async-done | bytes 262176 | tf_op jit(solution)/shard_map/all_to_all | solution.py:106
  79.9 0.5 convolution_convert_fusion
  80.5 0.4 copy-done.15
  80.9 0.6 convolution_convert_fusion.1
  81.6 12.1 %all_to_all.15 = bf16[4,64,512]{2,1,0:T(8,128)(2,1)S(1)} all-to-all(bf16[4,64,512]{2,1,0:T(8,128)(2,1)S(1)} %bitcast.32), channel_id=1, replica_groups=mesh['parts'=2,'band'=4,'feat'=2,'rep'=2] {'band'}, dimensions={0} | all-to-all | bytes 524288 | tf_op jit(solution)/shard_map/all_to_all | solution.py:112
  93.7 1.3 fusion.27
  95.1 92.6 %all-reduce.2.cloned.1.call-done = f32[512,512]{1,0:T(8,128)} async-done(((f32[512,512]{1,0:T(8,128)}), f32[512,512]{1,0:T(8,128)}) %all-reduce.2.cloned.1.call-update) | async-done | bytes 1048592 | tf_op jit(solution)/shard_map/psum | solution.py:122
  187.7 1.9 constant_dynamic-slice_fusion
  (48 shorter events, 1.8 us)
Async XLA Ops:
  7.2 72.8 %copy-start = (bf16[512,520]{0,1:T(8,128)(2,1)S(1)}, bf16[512,520]{0,1:T(8,128)(2,1)}, u32[]{:S(2)}) copy-start(bf16[512,520]{0,1:T(8,128)(2,1)} %param.31) | copy-start | bytes 1597444
  7.2 10.4 %copy-start.2 = (bf16[512,256]{1,0:T(8,128)(2,1)S(1)}, bf16[512,256]{1,0:T(8,128)(2,1)}, u32[]{:S(2)}) copy-start(bf16[512,256]{1,0:T(8,128)(2,1)} %param.23) | copy-start | bytes 786436
  17.6 8.3 %copy-start.9 = (s32[1,4,32]{2,1,0:T(4,128)S(1)}, s32[1,4,32]{2,1,0:T(4,128)}, u32[]{:S(2)}) copy-start(s32[1,4,32]{2,1,0:T(4,128)} %param.32) | copy-start | bytes 1540
  17.6 8.4 %copy-start.3 = (bf16[512,256]{1,0:T(8,128)(2,1)S(1)}, bf16[512,256]{1,0:T(8,128)(2,1)}, u32[]{:S(2)}) copy-start(bf16[512,256]{1,0:T(8,128)(2,1)} %param.25) | copy-start | bytes 786436
  26.0 7.4 %copy-start.1 = (bf16[256,520]{0,1:T(8,128)(2,1)S(1)}, bf16[256,520]{0,1:T(8,128)(2,1)}, u32[]{:S(2)}) copy-start(bf16[256,520]{0,1:T(8,128)(2,1)} %param.19) | copy-start | bytes 798724
  33.4 0.7 copy-start.8
  33.4 0.7 copy-start.13
  35.7 4.7 %copy-start.4 = (bf16[512,256]{1,0:T(8,128)(2,1)S(1)}, bf16[512,256]{1,0:T(8,128)(2,1)}, u32[]{:S(2)}) copy-start(bf16[512,256]{1,0:T(8,128)(2,1)} %param.26) | copy-start | bytes 786436
  35.7 29.4 %all-to-all-start = ((bf16[4,32,512]{2,1,0:T(8,128)(2,1)}), bf16[4,32,512]{2,1,0:T(8,128)(2,1)S(1)}, u32[]{:S(2)}, u32[]{:S(2)}) async-start(bf16[4,32,512]{2,1,0:T(8,128)(2,1)} %bitcast.1), calls=%async_computation | async-start | bytes 262144 | tf_op jit(solution)/shard_map/all_to_all | solution.py:88
  40.4 8.2 %copy-start.5 = (bf16[512,256]{1,0:T(8,128)(2,1)S(1)}, bf16[512,256]{1,0:T(8,128)(2,1)}, u32[]{:S(2)}) copy-start(bf16[512,256]{1,0:T(8,128)(2,1)} %param.28) | copy-start | bytes 786436
  48.7 7.9 %copy-start.10 = (s32[1,4,32]{2,1,0:T(4,128)S(1)}, s32[1,4,32]{2,1,0:T(4,128)}, u32[]{:S(2)}) copy-start(s32[1,4,32]{2,1,0:T(4,128)} %param.33) | copy-start | bytes 1540
  48.7 9.3 %copy-start.6 = (bf16[512,256]{1,0:T(8,128)(2,1)S(1)}, bf16[512,256]{1,0:T(8,128)(2,1)}, u32[]{:S(2)}) copy-start(bf16[512,256]{1,0:T(8,128)(2,1)} %param.30) | copy-start | bytes 786436
  56.5 0.7 copy-start.14
  57.2 0.7 copy-start.11
  58.0 7.2 %copy-start.7 = (bf16[128,512]{1,0:T(8,128)(2,1)S(1)}, bf16[128,512]{1,0:T(8,128)(2,1)}, u32[]{:S(2)}) copy-start(bf16[128,512]{1,0:T(8,128)(2,1)} %param.21) | copy-start | bytes 393220
  65.8 0.7 copy-start.16
  65.8 0.7 copy-start.17
  67.9 5.2 %copy-start.12 = (s32[1,4,64]{2,1,0:T(4,128)S(1)}, s32[1,4,64]{2,1,0:T(4,128)}, u32[]{:S(2)}) copy-start(s32[1,4,64]{2,1,0:T(4,128)} %param.36) | copy-start | bytes 3076
  67.9 12.1 %all-to-all-start.1 = ((bf16[4,64,512]{2,1,0:T(8,128)(2,1)}), bf16[4,64,512]{2,1,0:T(8,128)(2,1)S(1)}, u32[]{:S(2)}, u32[]{:S(2)}) async-start(bf16[4,64,512]{2,1,0:T(8,128)(2,1)} %bitcast.4), calls=%async_computation.1 | async-start | bytes 524288 | tf_op jit(solution)/shard_map/all_to_all | solution.py:106
  73.1 114.6 %all-reduce.2.cloned.1.call-start = ((), (), s32[]{:S(2)}) async-start(), calls=%async_computation.3 | async-start | bytes 2097152 | tf_op jit(solution)/shard_map/psum | solution.py:122
  79.9 1.0 copy-start.15
  80.9 0.7 copy-start.18
Sparse Core Ops, SparseCore 0:
  95.2 92.4 all-reduce.1
where the time goes:
time: 197 us; the launch traced here: 196 us
  waiting for transfers between devices  99.4 us (50%)
  blocking collectives  61.5 us (31%)
  between operations  14.1 us (7%)
  starting transfers between devices  9.9 us (5%)
  matrix products  6.78 us (3%)
  local copies, waits for them, and re-layouts  4.51 us (2%)
    psum x1, waiting for transfers between devices, local(): total = lax.psum(term, ('band', 'feat', 'rep'))  92.6 us
    all_gather x6, blocking collectives, project(): lax.all_gather(shard, 'feat', axis=1, tiled=True)  49.3 us
    all_to_all x1, blocking collectives, local(): lax.all_to_all(slot_cotangent.reshape(peers, -1, width), 'band', split_ax...  12.1 us
    all_to_all x1, waiting for transfers between devices, local(): lax.all_to_all(decode_message.reshape(peers, -1, width), 'band', split_ax...  6.77 us
    all_to_all x1, starting transfers between devices, local(): lax.all_to_all(decode_message.reshape(peers, -1, width), 'band', split_ax...  5.2 us
    all_to_all x1, starting transfers between devices, local(): lax.all_to_all(encode_message.reshape(peers, -1, width), 'band', split_ax...  4.7 us
  transfers between devices with their start and end apart: 3, of which 2 were waited for; matrix products, arithmetic and copies ran while one was open for 0% of the time, Pallas kernels for 0%

commit v1 on v0

v1 whole, which is shorter than its diff:
```python
import functools
import math

import jax
import jax.numpy as jnp
from jax import lax
from jax.experimental import pallas as pl
from jax.experimental.pallas import tpu as pltpu
from jax.sharding import PartitionSpec as P

eps_norm = 1e-05
MESH = pl.DeviceIdType.MESH
F32 = jnp.float32
BF16 = jnp.bfloat16
REACH = 2
HOPS = tuple(d for d in range(-REACH, REACH + 1) if d != 0)


def silu(v):
    return v / (1.0 + jnp.exp(-v))


def matmul(a, b):
    return jnp.dot(a, b, preferred_element_type=F32)


def matmul_tn(a, b):
    return lax.dot_general(a, b, (((0,), (0,)), ((), ())), preferred_element_type=F32)


def matmul_nt(a, b):
    return lax.dot_general(a, b, (((1,), (1,)), ((), ())), preferred_element_type=F32)


def onehot_rows(index_row, rows):
    at = lax.broadcasted_iota(jnp.int32, (rows, index_row.shape[1]), 0)
    return jnp.where(at == index_row, 1.0, 0.0).astype(BF16)


def forecaster(
    sizes,
    grid_in,
    target,
    mesh_in,
    embed_weight,
    encode_project,
    encode_attr_weight,
    encode_edge_weight,
    node_weight,
    node_gain,
    decode_project,
    decode_attr_weight,
    decode_edge_weight,
    out_weight,
    encode_senders,
    encode_receivers,
    encode_features,
    decode_senders,
    decode_receivers,
    decode_features,
    predicted_ref,
    gradient_ref,
    embed_full,
    weights_full,
    latent,
    encode_out,
    encode_in,
    decode_out,
    decode_in,
    collected,
    half_out,
    half_in,
    mine,
    pieces_out,
    pieces_in,
    final_out,
    final_in,
    w_send,
    w_recv,
    f_send,
    f_recv,
    e_send,
    e_recv,
    d_send,
    d_recv,
    h_sem,
    p_send,
    p_recv,
    g_send,
    g_recv,
):
    nb, nf, inside = sizes
    band, feat, rep = lax.axis_index("band"), lax.axis_index("feat"), lax.axis_index("rep")
    other = 1 - rep
    width = mesh_in.shape[1]
    columns = width // nf
    grid_rows, values = grid_in.shape
    mesh_rows = mesh_in.shape[0]
    group = nb * nf
    lane = nb * 2

    def in_range(b):
        return jnp.logical_and(b >= 0, b < nb)

    encode_in[...] = jnp.zeros_like(encode_in)
    decode_in[...] = jnp.zeros_like(decode_in)
    own = pl.ds(pl.multiple_of(feat * columns, columns), columns)
    padded = embed_full.shape[0]
    embed_full[pl.ds(padded - 32, 32), own] = jnp.zeros((32, columns), BF16)
    embed_full[pl.ds(0, values), own] = embed_weight[...]

    barrier = pltpu.get_barrier_semaphore()
    if inside:
        for db in range(nb):
            for df in range(nf):
                for dr in range(2):
                    if db + df + dr:
                        pl.semaphore_signal(
                            barrier,
                            inc=1,
                            device_id={
                                "band": lax.rem(band + db, nb),
                                "feat": lax.rem(feat + df, nf),
                                "rep": lax.rem(rep + dr, 2),
                            },
                            device_id_type=MESH,
                        )
    else:
        pl.semaphore_signal(barrier, inc=1, device_id={"rep": other}, device_id_type=MESH)
        for df in range(1, nf):
            pl.semaphore_signal(
                barrier, inc=1, device_id={"feat": lax.rem(feat + df, nf)}, device_id_type=MESH
            )
        for d in HOPS:
            @pl.when(in_range(band + d))
            def _():
                pl.semaphore_signal(barrier, inc=1, device_id={"band": band + d}, device_id_type=MESH)

    shards = (encode_project, encode_edge_weight, node_weight, decode_project, decode_edge_weight)
    for i, shard in enumerate(shards):
        weights_full[i, :, own] = shard[...]

    if inside:
        pl.semaphore_wait(barrier, group * 2 - 1)
    else:
        pl.semaphore_wait(barrier, nf)
        for d in HOPS:
            @pl.when(in_range(band + d))
            def _():
                pl.semaphore_wait(barrier, 1)

    def part(i, r, f):
        cols = pl.ds(pl.multiple_of(f * columns, columns), columns)
        if i == 0:
            h = padded // 2
            return embed_full.at[pl.ds(pl.multiple_of(r * h, 16), h), cols]
        h = width // 2
        return weights_full.at[i - 1, pl.ds(pl.multiple_of(r * h, 16), h), cols]

    def across(i, off):
        view = part(i, rep, feat)
        return pltpu.make_async_remote_copy(
            src_ref=view,
            dst_ref=view,
            send_sem=w_send.at[i, off - 1],
            recv_sem=w_recv.at[i, off - 1],
            device_id={"feat": lax.rem(feat + off, nf)},
            device_id_type=MESH,
        )

    def handed(i, off):
        view = part(i, rep, lax.rem(feat + nf - off, nf))
        return pltpu.make_async_remote_copy(
            src_ref=view,
            dst_ref=view,
            send_sem=f_send.at[i, off - 1],
            recv_sem=f_recv.at[i, off - 1],
            device_id={"rep": other},
            device_id_type=MESH,
        )

    def hand_on(i):
        for off in range(1, nf):
            across(i, off).wait_recv()
            handed(i, off).start()

    def ready(i):
        for off in range(1, nf):
            handed(i, off).wait_recv()

    for i in range(6):
        for off in range(1, nf):
            across(i, off).start()

    def message(out, arrive, send_sem, recv_sem, cap, k):
        return pltpu.make_async_remote_copy(
            src_ref=out.at[pl.ds(pl.multiple_of((band + HOPS[k]) * cap, cap), cap)],
            dst_ref=arrive.at[pl.ds(pl.multiple_of(band * cap, cap), cap)],
            send_sem=send_sem.at[k],
            recv_sem=recv_sem.at[k],
            device_id={"band": band + HOPS[k]},
            device_id_type=MESH,
        )

    def send_all(out, arrive, send_sem, recv_sem, cap):
        for k, d in enumerate(HOPS):
            @pl.when(in_range(band + d))
            def _():
                message(out, arrive, send_sem, recv_sem, cap, k).start()
        here = pl.ds(pl.multiple_of(band * cap, cap), cap)
        arrive[here, :] = out[here, :]

    def recv_all(out, arrive, send_sem, recv_sem, cap):
        for k, d in enumerate(HOPS):
            @pl.when(in_range(band - d))
            def _():
                pltpu.make_async_remote_copy(
                    src_ref=out.at[pl.ds(0, cap)],
                    dst_ref=arrive.at[pl.ds(pl.multiple_of((band - d) * cap, cap), cap)],
                    send_sem=send_sem.at[k],
                    recv_sem=recv_sem.at[k],
                    device_id={"band": band - d},
                    device_id_type=MESH,
                ).wait_recv()

    def sent_all(out, arrive, send_sem, recv_sem, cap):
        for k, d in enumerate(HOPS):
            @pl.when(in_range(band + d))
            def _():
                message(out, arrive, send_sem, recv_sem, cap, k).wait_send()

    cap_e = encode_out.shape[0] // nb
    cap_d = decode_out.shape[0] // nb
    enc = (encode_out, encode_in, e_send, e_recv, cap_e)
    dec = (decode_out, decode_in, d_send, d_recv, cap_d)

    encode_attr = matmul_tn(encode_features[0], encode_attr_weight[...])
    encode_pick = onehot_rows(encode_senders[...], grid_rows)
    hand_on(0)
    ready(0)
    latent[...] = silu(matmul(grid_in[...], embed_full[pl.ds(0, values), :])).astype(BF16)
    hand_on(1)
    ready(1)
    grid_project = matmul(latent[...], weights_full[0]).astype(BF16)
    encode_out[...] = silu(matmul_tn(encode_pick, grid_project) + encode_attr).astype(BF16)
    send_all(*enc)

    hand_on(2)
    decode_attr = matmul_tn(decode_features[0], decode_attr_weight[...])
    decode_pick = onehot_rows(decode_senders[...], mesh_rows)
    encode_collect = onehot_rows(encode_receivers[...], mesh_rows)
    decode_collect = onehot_rows(decode_receivers[...], grid_rows)
    recv_all(*enc)
    gathered = matmul(encode_collect, encode_in[...]).astype(BF16)
    ready(2)
    aggregated = matmul(gathered, weights_full[1]).astype(BF16)
    hand_on(3)
    ready(3)
    update = mesh_in[...].astype(F32) + matmul(aggregated, weights_full[2])
    hand_on(4)
    centered = update - jnp.mean(update, axis=-1, keepdims=True)
    spread = jnp.mean(centered * centered, axis=-1, keepdims=True)
    mesh_latent = (node_gain[...].astype(F32) * centered * lax.rsqrt(spread + eps_norm)).astype(BF16)
    ready(4)
    mesh_project = matmul(mesh_latent, weights_full[3]).astype(BF16)
    decode_out[...] = silu(matmul_tn(decode_pick, mesh_project) + decode_attr).astype(BF16)
    send_all(*dec)
    hand_on(5)
    ready(5)
    recv_all(*dec)

    collected[...] = matmul(decode_collect, decode_in[...]).astype(BF16)
    incoming = matmul(collected[...], weights_full[4])
    decoded = (latent[...].astype(F32) + incoming).astype(BF16)
    predicted = matmul(decoded, out_weight[...]).astype(BF16)
    predicted_ref[...] = predicted
    scale = math.sqrt(grid_rows * nb * nf * 2)
    error = ((predicted.astype(F32) - target[...].astype(F32)) / scale).astype(BF16)
    cotangent = matmul_nt(error, out_weight[...]).astype(BF16)

    if not inside:
        gradient_ref[...] = matmul_tn(collected[...], cotangent)
    else:
        half = width // 2
        rows = half // nb

        def term(r):
            return matmul_tn(
                collected[:, pl.ds(pl.multiple_of(r * half, half), half)], cotangent
            )

        half_out[...] = term(other).astype(BF16)
        swap = pltpu.make_async_remote_copy(
            src_ref=half_out,
            dst_ref=half_in,
            send_sem=h_sem.at[0],
            recv_sem=h_sem.at[1],
            device_id={"rep": other},
            device_id_type=MESH,
        )
        swap.start()
        mine[...] = term(rep)
        swap.wait_recv()
        summed = mine[...] + half_in[...].astype(F32)
        mine[...] = summed
        pieces_out[...] = summed.astype(BF16)
        place = band * nf + feat

        def piece(k):
            to = lax.rem(place + k, group)
            tb, tf = lax.div(to, nf), lax.rem(to, nf)
            return pltpu.make_async_remote_copy(
                src_ref=pieces_out.at[
                    pl.ds(pl.multiple_of(tb * rows, 16), rows),
                    pl.ds(pl.multiple_of(tf * columns, columns), columns),
                ],
                dst_ref=pieces_in.at[k - 1],
                send_sem=p_send.at[k - 1],
                recv_sem=p_recv.at[k - 1],
                device_id={"band": tb, "feat": tf},
                device_id_type=MESH,
            )

        for k in range(1, group):
            piece(k).start()
        total = mine[pl.ds(pl.multiple_of(band * rows, 16), rows), own]
        for k in range(1, group):
            piece(k).wait_recv()
            total = total + pieces_in[k - 1].astype(F32)
        final_out[...] = total.astype(BF16)
        spot = band * 2 + rep

        def final(k):
            to = lax.rem(spot + k, lane)
            return pltpu.make_async_remote_copy(
                src_ref=final_out,
                dst_ref=final_in.at[k - 1],
                send_sem=g_send.at[k - 1],
                recv_sem=g_recv.at[k - 1],
                device_id={"band": lax.div(to, 2), "rep": lax.rem(to, 2)},
                device_id_type=MESH,
            )

        def rows_of(s):
            start = lax.rem(s, 2) * half + lax.div(s, 2) * rows
            return pl.ds(pl.multiple_of(start, 16), rows)

        for k in range(1, lane):
            final(k).start()
        gradient_ref[rows_of(spot), :] = final_out[...].astype(F32)
        for k in range(1, lane):
            final(k).wait_recv()
            gradient_ref[rows_of(lax.rem(spot + lane - k, lane)), :] = final_in[k - 1].astype(F32)

    for i in range(6):
        for off in range(1, nf):
            across(i, off).wait_send()
            handed(i, off).wait_send()
    sent_all(*enc)
    sent_all(*dec)
    if inside:
        swap.wait_send()
        for k in range(1, group):
            piece(k).wait_send()
        for k in range(1, lane):
            final(k).wait_send()


def local(sizes, *args):
    nb, nf, inside = sizes
    args = list(args)
    grid_in, mesh_in = args[0], args[2]
    width = mesh_in.shape[1]
    columns = width // nf
    args[8] = args[8].reshape(1, width)
    for at in (13, 14, 16, 17):
        args[at] = args[at].reshape(1, -1)
    cap_e = args[13].shape[1]
    cap_d = args[16].shape[1]
    half = width // 2
    rows = half // nb if inside else 16
    padded = -(-grid_in.shape[1] // 32) * 32
    slots = max(nf - 1, 1)
    dma = pltpu.SemaphoreType.DMA
    group, lane = (nb * nf, nb * 2) if inside else (2, 2)
    predicted, gradient = pl.pallas_call(
        functools.partial(forecaster, sizes),
        out_shape=(
            jax.ShapeDtypeStruct(grid_in.shape, BF16),
            jax.ShapeDtypeStruct((width, columns if inside else width), F32),
        ),
        in_specs=[pl.BlockSpec(memory_space=pltpu.VMEM)] * len(args),
        out_specs=(pl.BlockSpec(memory_space=pltpu.VMEM),) * 2,
        scratch_shapes=[
            pltpu.VMEM((padded, width), BF16),
            pltpu.VMEM((5, width, width), BF16),
            pltpu.VMEM((grid_in.shape[0], width), BF16),
            pltpu.VMEM((cap_e, width), BF16),
            pltpu.VMEM((cap_e, width), BF16),
            pltpu.VMEM((cap_d, width), BF16),
            pltpu.VMEM((cap_d, width), BF16),
            pltpu.VMEM((grid_in.shape[0], width), BF16),
            pltpu.VMEM((half, width), BF16),
            pltpu.VMEM((half, width), BF16),
            pltpu.VMEM((half, width), F32),
            pltpu.VMEM((half, width), BF16),
            pltpu.VMEM((group - 1, rows, columns), BF16),
            pltpu.VMEM((rows, columns), BF16),
            pltpu.VMEM((lane - 1, rows, columns), BF16),
            dma((6, slots)),
            dma((6, slots)),
            dma((6, slots)),
            dma((6, slots)),
            dma((len(HOPS),)),
            dma((len(HOPS),)),
            dma((len(HOPS),)),
            dma((len(HOPS),)),
            dma((2,)),
            dma((group - 1,)),
            dma((group - 1,)),
            dma((lane - 1,)),
            dma((lane - 1,)),
        ],
        compiler_params=pltpu.CompilerParams(
            collective_id=0, has_side_effects=True, vmem_limit_bytes=48 * 1024 * 1024
        ),
    )(*args)
    if not inside:
        total = lax.psum(gradient, ("band", "feat", "rep"))
        gradient = lax.dynamic_slice_in_dim(total, lax.axis_index("feat") * columns, columns, 1)
    return (predicted, gradient)


def solution(mesh):
    nb, nf = mesh.shape["band"], mesh.shape["feat"]
    inside = nb <= 8 and nf <= 2
    slab = ("parts", "band", "feat", "rep")
    return jax.shard_map(
        functools.partial(local, (nb, nf, inside)),
        mesh=mesh,
        in_specs=(
            P(slab, None),
            P(slab, None),
            P(slab, None),
            P(None, "feat"),
            P(None, "feat"),
            P(),
            P(None, "feat"),
            P(None, "feat"),
            P(),
            P(None, "feat"),
            P(),
            P(None, "feat"),
            P(),
        )
        + (P(slab, None, None),) * 6,
        out_specs=(P(slab, None), P("parts", "feat")),
        check_vma=False,
    )
```

time: 197 us -> 53.7 us (0.27)
  waiting for transfers between devices: 99.4 us -> 0 us
  blocking collectives: 61.5 us -> 0 us
  Pallas kernels: 0 us -> 44.9 us
  between operations: 14.1 us -> 0.78 us
  starting transfers between devices: 9.9 us -> 0 us
  matrix products: 6.78 us -> 0 us
  local copies, waits for them, and re-layouts: 4.51 us -> 7.7 us
    psum x1 -> x0, waiting for transfers between devices: 92.6 us -> none  [local(): total = lax.psum(term, ('band', 'feat', 'rep'))]
    all_gather x6 -> x0, blocking collectives: 49.3 us -> none  [project(): lax.all_gather(shard, 'feat', axis=1, tiled=True)]
    pallas_call x0 -> x1, Pallas kernels: none -> 44.9 us  [local(): pl.pallas_call(functools.partial(forecaster, sizes), out_shape=(jax.Shape...]
    all_to_all x1 -> x0, blocking collectives: 12.1 us -> none  [local(): lax.all_to_all(slot_cotangent.reshape(peers, -1, width), 'band', split_ax...]
    all_to_all x2 -> x0, starting transfers between devices: 9.9 us -> none  [the longest x1 5.2 us: local(): lax.all_to_all(decode_message.reshape(peers, -1, width), 'band', split_ax...]
    dot_general x11 -> x0, matrix products: 6.78 us -> none  [the longest x4 2.69 us: project(): jnp.dot(activation, lax.all_gather(shard, 'feat', axis=1, tiled=True), pr...]
    all_to_all x2 -> x0, waiting for transfers between devices: 6.77 us -> none  [the longest x1 6.77 us: local(): lax.all_to_all(decode_message.reshape(peers, -1, width), 'band', split_ax...]
    unnamed x38, local copies, waits for them, and re-layouts: 2.31 us -> 5.83 us
  transfers between devices with their start and end apart: 3 -> 0, of which waited for: 2 -> 0; matrix products, arithmetic and copies ran while one was open for 0% -> 0% of each run, Pallas kernels for 0% -> 0%
where the time goes in v1:
time: 53.7 us; the launch traced here: 53.4 us
  Pallas kernels  44.9 us (84%)
  local copies, waits for them, and re-layouts  7.7 us (14%)
  between operations  0.78 us (1%)
    pallas_call x1, Pallas kernels, local(): pl.pallas_call(functools.partial(forecaster, sizes), out_shape=(jax.Shape...  44.9 us
    unnamed x38, local copies, waits for them, and re-layouts  5.83 us

profile of v1, /device:TPU:0, one launch (start us, length us, event | category | flops | bytes accessed | tf_op | source)
XLA Modules:
  0.0 53.4 jit_solution(13641341382739593401)
XLA Ops:
  0.7 0.8 %reshape.20.encode_senders = s32[1,128]{1,0:T(1,128)S(1)} reshape(s32[1,4,32]{2,1,0:T(4,128)} %param.32) | data formatting | bytes 1024 | tf_op jit(solution)/shard_map/reshape | solution.py:377
  1.4 0.1 reshape.21.encode_receivers
  1.5 0.1 reshape.22.decode_senders
  1.6 0.6 %copy-done.15 = s32[1,4,64]{2,1,0:T(4,128)S(1)} copy-done((s32[1,4,64]{2,1,0:T(4,128)S(1)}, s32[1,4,64]{2,1,0:T(4,128)}, u32[]{:S(2)}) %copy-start.15) | copy-done | bytes 1048
  2.2 0.1 reshape.23.decode_receivers
  2.3 1.2 %copy.21.grid_in = bf16[256,520]{1,0:T(8,128)(2,1)S(1)} copy(bf16[256,520]{0,1:T(8,128)(2,1)} %param.19) | data formatting | bytes 532480 | tf_op args[0]
  3.5 0.0 copy-start.4
  3.5 0.2 copy.22.target
  3.7 0.0 copy-start
  3.8 0.0 copy-start.1
  3.8 0.0 copy-start.2
  3.8 0.0 copy-start.7
  3.8 0.0 copy-start.8
  3.8 0.3 copy.23.out_weight
  4.1 0.3 copy-done.4
  4.5 0.2 copy-done
  4.7 0.1 copy-done.1
  4.8 0.1 copy-done.2
  4.9 0.1 copy-done.3
  5.0 0.9 %copy-done.5 = bf16[512,256]{1,0:T(8,128)(2,1)S(1)} copy-done((bf16[512,256]{1,0:T(8,128)(2,1)S(1)}, bf16[512,256]{1,0:T(8,128)(2,1)}, u32[]{:S(2)}) %copy-start.5) | copy-done | bytes 262168
  5.9 0.9 %copy-done.6 = bf16[128,512]{1,0:T(8,128)(2,1)S(1)} copy-done((bf16[128,512]{1,0:T(8,128)(2,1)S(1)}, bf16[128,512]{1,0:T(8,128)(2,1)}, u32[]{:S(2)}) %copy-start.6) | copy-done | bytes 131096
  6.8 44.9 %shard_map.194 = (bf16[256,520]{1,0:T(8,128)(2,1)S(1)}, f32[512,256]{1,0:T(8,128)S(1)}) custom-call(bf16[256,520]{1,0:T(8,128)(2,1)S(1)} %copy.21.grid_in, bf16[256,520]{1,0:T(8,128)(2,1)S(1)} %copy.22.target, bf16[128,512]{1,0:T(8,128)(2,1)S(1)} %copy-done.6, bf16[520,256]{1,0:T(8,128)(2,1)S(1)} %copy-done, bf16[512,256]{1,0:T(8,128)(2,1)S(1)} %copy-done.1, ...), custom_call_target="tpu_custom_call" | custom-call | tf_op jit(solution)/shard_map/pallas_call | solution.py:386
  51.8 0.9 %copy.24 = bf16[256,520]{0,1:T(8,128)(2,1)} copy(bf16[256,520]{1,0:T(8,128)(2,1)S(1)} %get-tuple-element.2) | data formatting | bytes 532480 | tf_op jit(solution)/shard_map/pallas_call | solution.py:386
  52.6 0.8 %copy.26 = f32[512,256]{1,0:T(8,128)} copy(f32[512,256]{1,0:T(8,128)S(1)} %get-tuple-element.7) | data formatting | bytes 1048576
  (21 shorter events, 0.1 us)
Async XLA Ops:
  0.6 0.8 %copy-start.13 = (s32[1,4,32]{2,1,0:T(4,128)S(1)}, s32[1,4,32]{2,1,0:T(4,128)}, u32[]{:S(2)}) copy-start(s32[1,4,32]{2,1,0:T(4,128)} %param.33) | copy-start | bytes 1540
  0.6 0.9 %copy-start.14 = (s32[1,4,64]{2,1,0:T(4,128)S(1)}, s32[1,4,64]{2,1,0:T(4,128)}, u32[]{:S(2)}) copy-start(s32[1,4,64]{2,1,0:T(4,128)} %param.35) | copy-start | bytes 3076
  1.5 0.7 %copy-start.15 = (s32[1,4,64]{2,1,0:T(4,128)S(1)}, s32[1,4,64]{2,1,0:T(4,128)}, u32[]{:S(2)}) copy-start(s32[1,4,64]{2,1,0:T(4,128)} %param.36) | copy-start | bytes 3076
  1.5 0.8 %copy-start.16 = (bf16[512]{0:T(512)(128)(2,1)S(1)}, bf16[512]{0:T(512)(128)(2,1)}, u32[]{:S(2)}) copy-start(bf16[512]{0:T(512)(128)(2,1)} %param.27) | copy-start | bytes 3076
  2.2 1.3 %copy-start.12 = (bf16[256,520]{0,1:T(8,128)(2,1)S(1)}, bf16[256,520]{0,1:T(8,128)(2,1)}, u32[]{:S(2)}) copy-start(bf16[256,520]{0,1:T(8,128)(2,1)} %param.20) | copy-start | bytes 798724
  2.3 1.4 %copy-start.11 = (bf16[512,520]{0,1:T(8,128)(2,1)S(1)}, bf16[512,520]{0,1:T(8,128)(2,1)}, u32[]{:S(2)}) copy-start(bf16[512,520]{0,1:T(8,128)(2,1)} %param.31) | copy-start | bytes 1597444
  3.5 1.0 %copy-start.4 = (bf16[512,256]{1,0:T(8,128)(2,1)S(1)}, bf16[512,256]{1,0:T(8,128)(2,1)}, u32[]{:S(2)}) copy-start(bf16[512,256]{1,0:T(8,128)(2,1)} %decode_project.1) | copy-start | bytes 786436
  3.7 1.0 %copy-start = (bf16[520,256]{1,0:T(8,128)(2,1)S(1)}, bf16[520,256]{1,0:T(8,128)(2,1)}, u32[]{:S(2)}) copy-start(bf16[520,256]{1,0:T(8,128)(2,1)} %embed_weight.1) | copy-start | bytes 798724
  3.8 1.0 %copy-start.1 = (bf16[512,256]{1,0:T(8,128)(2,1)S(1)}, bf16[512,256]{1,0:T(8,128)(2,1)}, u32[]{:S(2)}) copy-start(bf16[512,256]{1,0:T(8,128)(2,1)} %encode_project.1) | copy-start | bytes 786436
  3.8 1.1 %copy-start.2 = (bf16[512,256]{1,0:T(8,128)(2,1)S(1)}, bf16[512,256]{1,0:T(8,128)(2,1)}, u32[]{:S(2)}) copy-start(bf16[512,256]{1,0:T(8,128)(2,1)} %encode_edge_weight.1) | copy-start | bytes 786436
  3.8 1.2 %copy-start.3 = (bf16[512,256]{1,0:T(8,128)(2,1)S(1)}, bf16[512,256]{1,0:T(8,128)(2,1)}, u32[]{:S(2)}) copy-start(bf16[512,256]{1,0:T(8,128)(2,1)} %node_weight.1) | copy-start | bytes 786436
  3.8 1.2 %copy-start.7 = (bf16[4,512]{1,0:T(4,128)(2,1)S(1)}, bf16[4,512]{1,0:T(4,128)(2,1)}, u32[]{:S(2)}) copy-start(bf16[4,512]{1,0:T(4,128)(2,1)} %encode_attr_weight.1) | copy-start | bytes 12292
  3.8 1.2 %copy-start.8 = (bf16[4,512]{1,0:T(4,128)(2,1)S(1)}, bf16[4,512]{1,0:T(4,128)(2,1)}, u32[]{:S(2)}) copy-start(bf16[4,512]{1,0:T(4,128)(2,1)} %decode_attr_weight.1) | copy-start | bytes 12292
  3.8 1.1 %copy-start.9 = (bf16[1,4,256]{2,1,0:T(4,128)(2,1)S(1)}, bf16[1,4,256]{2,1,0:T(4,128)(2,1)}, u32[]{:S(2)}) copy-start(bf16[1,4,256]{2,1,0:T(4,128)(2,1)} %decode_features.1) | copy-start | bytes 6148
  3.8 1.1 %copy-start.10 = (bf16[1,4,128]{2,1,0:T(4,128)(2,1)S(1)}, bf16[1,4,128]{2,1,0:T(4,128)(2,1)}, u32[]{:S(2)}) copy-start(bf16[1,4,128]{2,1,0:T(4,128)(2,1)} %encode_features.1) | copy-start | bytes 3076
  5.0 1.0 %copy-start.5 = (bf16[512,256]{1,0:T(8,128)(2,1)S(1)}, bf16[512,256]{1,0:T(8,128)(2,1)}, u32[]{:S(2)}) copy-start(bf16[512,256]{1,0:T(8,128)(2,1)} %decode_edge_weight.1) | copy-start | bytes 786436
  5.9 0.9 %copy-start.6 = (bf16[128,512]{1,0:T(8,128)(2,1)S(1)}, bf16[128,512]{1,0:T(8,128)(2,1)}, u32[]{:S(2)}) copy-start(bf16[128,512]{1,0:T(8,128)(2,1)} %mesh_in.1) | copy-start | bytes 393220

commit v2 on v1

--- a/solution.py
+++ b/solution.py
@@ -39,18 +39,34 @@
 
 def forecaster(
     sizes,
+    grid_in_hbm,
+    target_hbm,
+    mesh_in_hbm,
+    embed_hbm,
+    encode_project_hbm,
+    encode_attr_hbm,
+    encode_edge_hbm,
+    node_weight_hbm,
+    node_gain_hbm,
+    decode_project_hbm,
+    decode_attr_hbm,
+    decode_edge_hbm,
+    out_weight_hbm,
+    encode_senders_hbm,
+    encode_receivers_hbm,
+    encode_features_hbm,
+    decode_senders_hbm,
+    decode_receivers_hbm,
+    decode_features_hbm,
+    predicted_ref,
+    gradient_ref,
     grid_in,
     target,
     mesh_in,
-    embed_weight,
-    encode_project,
+    embed_own,
     encode_attr_weight,
-    encode_edge_weight,
-    node_weight,
     node_gain,
-    decode_project,
     decode_attr_weight,
-    decode_edge_weight,
     out_weight,
     encode_senders,
     encode_receivers,
@@ -58,8 +74,6 @@
     decode_senders,
     decode_receivers,
     decode_features,
-    predicted_ref,
-    gradient_ref,
     embed_full,
     weights_full,
     latent,
@@ -75,8 +89,12 @@
     pieces_in,
     final_out,
     final_in,
+    load_sem,
+    own_sem,
     w_send,
     w_recv,
+    y_send,
+    y_recv,
     f_send,
     f_recv,
     e_send,
@@ -89,78 +107,125 @@
     g_send,
     g_recv,
 ):
-    nb, nf, inside = sizes
+    npart, nb, nf, inside = sizes
     band, feat, rep = lax.axis_index("band"), lax.axis_index("feat"), lax.axis_index("rep")
+    side = lax.axis_index("parts")
     other = 1 - rep
     width = mesh_in.shape[1]
     columns = width // nf
-    grid_rows, values = grid_in.shape
+    values, grid_rows = grid_in.shape
     mesh_rows = mesh_in.shape[0]
     group = nb * nf
     lane = nb * 2
+    shares = npart * 2
 
     def in_range(b):
         return jnp.logical_and(b >= 0, b < nb)
 
-    encode_in[...] = jnp.zeros_like(encode_in)
-    decode_in[...] = jnp.zeros_like(decode_in)
-    own = pl.ds(pl.multiple_of(feat * columns, columns), columns)
-    padded = embed_full.shape[0]
-    embed_full[pl.ds(padded - 32, 32), own] = jnp.zeros((32, columns), BF16)
-    embed_full[pl.ds(0, values), own] = embed_weight[...]
+    def greet(peer):
+        pl.semaphore_signal(barrier, inc=1, device_id=peer, device_id_type=MESH)
 
     barrier = pltpu.get_barrier_semaphore()
+    for dy in range(1, npart):
+        greet({"parts": lax.rem(side + dy, npart)})
     if inside:
         for db in range(nb):
             for df in range(nf):
                 for dr in range(2):
-                    if db + df + dr:
-                        pl.semaphore_signal(
-                            barrier,
-                            inc=1,
-                            device_id={
+                    if (db or df or dr) and not (df and dr):
+                        greet(
+                            {
                                 "band": lax.rem(band + db, nb),
                                 "feat": lax.rem(feat + df, nf),
                                 "rep": lax.rem(rep + dr, 2),
-                            },
-                            device_id_type=MESH,
+                            }
                         )
     else:
-        pl.semaphore_signal(barrier, inc=1, device_id={"rep": other}, device_id_type=MESH)
+        greet({"rep": other})
         for df in range(1, nf):
-            pl.semaphore_signal(
-                barrier, inc=1, device_id={"feat": lax.rem(feat + df, nf)}, device_id_type=MESH
-            )
+            greet({"feat": lax.rem(feat + df, nf)})
         for d in HOPS:
             @pl.when(in_range(band + d))
             def _():
-                pl.semaphore_signal(barrier, inc=1, device_id={"band": band + d}, device_id_type=MESH)
-
-    shards = (encode_project, encode_edge_weight, node_weight, decode_project, decode_edge_weight)
+                greet({"band": band + d})
+
+    loads = {}
+    for k, (name, src, dst) in enumerate(
+        (
+            ("embed", embed_hbm, embed_own),
+            ("grid", grid_in_hbm, grid_in),
+            ("es", encode_senders_hbm, encode_senders),
+            ("ef", encode_features_hbm, encode_features),
+            ("ea", encode_attr_hbm, encode_attr_weight),
+            ("er", encode_receivers_hbm, encode_receivers),
+            ("mesh", mesh_in_hbm, mesh_in),
+            ("gain", node_gain_hbm, node_gain),
+            ("ds", decode_senders_hbm, decode_senders),
+            ("df", decode_features_hbm, decode_features),
+            ("da", decode_attr_hbm, decode_attr_weight),
+            ("dr", decode_receivers_hbm, decode_receivers),
+            ("out", out_weight_hbm, out_weight),
+            ("target", target_hbm, target),
+        )
+    ):
+        loads[name] = pltpu.make_async_copy(src, dst, load_sem.at[k])
+        loads[name].start()
+
+    def loaded(*names):
+        for name in names:
+            loads[name].wait()
+
+    own = pl.ds(pl.multiple_of(feat * columns, columns), columns)
+    padded = embed_full.shape[0]
+    shards = (
+        encode_project_hbm,
+        encode_edge_hbm,
+        node_weight_hbm,
+        decode_project_hbm,
+        decode_edge_hbm,
+    )
+    owns = []
     for i, shard in enumerate(shards):
-        weights_full[i, :, own] = shard[...]
+        owns.append(pltpu.make_async_copy(shard, weights_full.at[i, :, own], own_sem.at[i]))
+        owns[i].start()
+    cap_e = encode_out.shape[0] // nb
+    cap_d = decode_out.shape[0] // nb
+    for p in range(nb):
+        @pl.when(jnp.logical_or(band - p > REACH, p - band > REACH))
+        def _():
+            encode_in[pl.ds(p * cap_e, cap_e), :] = jnp.zeros((cap_e, width), BF16)
+            decode_in[pl.ds(p * cap_d, cap_d), :] = jnp.zeros((cap_d, width), BF16)
+    base = values // 32 * 32
+    embed_full[pl.ds(base, padded - base), own] = jnp.zeros((padded - base, columns), BF16)
+    loaded("embed")
+    embed_full[pl.ds(0, values), own] = embed_own[...]
 
     if inside:
-        pl.semaphore_wait(barrier, group * 2 - 1)
+        pl.semaphore_wait(barrier, npart - 1 + nb * (nf + 1) - 1)
     else:
-        pl.semaphore_wait(barrier, nf)
+        pl.semaphore_wait(barrier, npart - 1 + nf)
         for d in HOPS:
             @pl.when(in_range(band + d))
             def _():
                 pl.semaphore_wait(barrier, 1)
 
-    def part(i, r, f):
+    def cut(i):
+        return (padded if i == 0 else width) // shares
+
+    def spot_of(i, y, r):
+        h = cut(i)
+        return pl.ds(pl.multiple_of((y * 2 + r) * h, 16), h)
+
+    def part(i, y, r, f):
         cols = pl.ds(pl.multiple_of(f * columns, columns), columns)
         if i == 0:
-            h = padded // 2
-            return embed_full.at[pl.ds(pl.multiple_of(r * h, 16), h), cols]
-        h = width // 2
-        return weights_full.at[i - 1, pl.ds(pl.multiple_of(r * h, 16), h), cols]
+            return embed_full.at[spot_of(i, y, r), cols]
+        return weights_full.at[i - 1, spot_of(i, y, r), cols]
 
     def across(i, off):
-        view = part(i, rep, feat)
+        view = part(i, side, rep, feat)
         return pltpu.make_async_remote_copy(
-            src_ref=view,
+            src_ref=view if i == 0 else shards[i - 1].at[spot_of(i, side, rep), :],
             dst_ref=view,
             send_sem=w_send.at[i, off - 1],
             recv_sem=w_recv.at[i, off - 1],
@@ -168,13 +233,24 @@
             device_id_type=MESH,
         )
 
-    def handed(i, off):
-        view = part(i, rep, lax.rem(feat + nf - off, nf))
+    def traded(i, off, dy):
+        view = part(i, side, rep, lax.rem(feat + nf - off, nf))
         return pltpu.make_async_remote_copy(
             src_ref=view,
             dst_ref=view,
-            send_sem=f_send.at[i, off - 1],
-            recv_sem=f_recv.at[i, off - 1],
+            send_sem=y_send.at[i, off - 1, dy - 1],
+            recv_sem=y_recv.at[i, off - 1, dy - 1],
+            device_id={"parts": lax.rem(side + dy, npart)},
+            device_id_type=MESH,
+        )
+
+    def handed(i, off, dy):
+        view = part(i, lax.rem(side + npart - dy, npart), rep, lax.rem(feat + nf - off, nf))
+        return pltpu.make_async_remote_copy(
+            src_ref=view,
+            dst_ref=view,
+            send_sem=f_send.at[i, off - 1, dy],
+            recv_sem=f_recv.at[i, off - 1, dy],
             device_id={"rep": other},
             device_id_type=MESH,
         )
@@ -182,11 +258,22 @@
     def hand_on(i):
         for off in range(1, nf):
             across(i, off).wait_recv()
-            handed(i, off).start()
+            for dy in range(1, npart):
+                traded(i, off, dy).start()
+            handed(i, off, 0).start()
+
+    def hand_over(i):
+        for off in range(1, nf):
+            for dy in range(1, npart):
+                traded(i, off, dy).wait_recv()
+                handed(i, off, dy).start()
 
     def ready(i):
+        if i:
+            owns[i - 1].wait()
         for off in range(1, nf):
-            handed(i, off).wait_recv()
+            for dy in range(npart):
+                handed(i, off, dy).wait_recv()
 
     for i in range(6):
         for off in range(1, nf):
@@ -229,35 +316,45 @@
             def _():
                 message(out, arrive, send_sem, recv_sem, cap, k).wait_send()
 
-    cap_e = encode_out.shape[0] // nb
-    cap_d = decode_out.shape[0] // nb
     enc = (encode_out, encode_in, e_send, e_recv, cap_e)
     dec = (decode_out, decode_in, d_send, d_recv, cap_d)
 
+    def slot_row(blocks):
+        return jnp.concatenate([blocks[0, pl.ds(p, 1), :] for p in range(nb)], axis=1)
+
+    loaded("ef", "ea", "es", "grid")
     encode_attr = matmul_tn(encode_features[0], encode_attr_weight[...])
-    encode_pick = onehot_rows(encode_senders[...], grid_rows)
+    encode_pick = onehot_rows(slot_row(encode_senders), grid_rows)
     hand_on(0)
+    hand_on(1)
+    hand_over(0)
     ready(0)
-    latent[...] = silu(matmul(grid_in[...], embed_full[pl.ds(0, values), :])).astype(BF16)
-    hand_on(1)
+    latent[...] = silu(matmul_tn(grid_in[...], embed_full[pl.ds(0, values), :])).astype(BF16)
+    hand_over(1)
+    hand_on(2)
     ready(1)
     grid_project = matmul(latent[...], weights_full[0]).astype(BF16)
     encode_out[...] = silu(matmul_tn(encode_pick, grid_project) + encode_attr).astype(BF16)
     send_all(*enc)
 
-    hand_on(2)
+    hand_over(2)
+    hand_on(3)
+    loaded("df", "da", "ds", "er", "dr")
     decode_attr = matmul_tn(decode_features[0], decode_attr_weight[...])
-    decode_pick = onehot_rows(decode_senders[...], mesh_rows)
-    encode_collect = onehot_rows(encode_receivers[...], mesh_rows)
-    decode_collect = onehot_rows(decode_receivers[...], grid_rows)
+    decode_pick = onehot_rows(slot_row(decode_senders), mesh_rows)
+    encode_collect = onehot_rows(slot_row(encode_receivers), mesh_rows)
+    decode_collect = onehot_rows(slot_row(decode_receivers), grid_rows)
+    hand_over(3)
+    hand_on(4)
     recv_all(*enc)
     gathered = matmul(encode_collect, encode_in[...]).astype(BF16)
     ready(2)
     aggregated = matmul(gathered, weights_full[1]).astype(BF16)
-    hand_on(3)
+    loaded("mesh", "gain")
     ready(3)
     update = mesh_in[...].astype(F32) + matmul(aggregated, weights_full[2])
-    hand_on(4)
+    hand_over(4)
+    hand_on(5)
     centered = update - jnp.mean(update, axis=-1, keepdims=True)
     spread = jnp.mean(centered * centered, axis=-1, keepdims=True)
     mesh_latent = (node_gain[...].astype(F32) * centered * lax.rsqrt(spread + eps_norm)).astype(BF16)
@@ -265,18 +362,19 @@
     mesh_project = matmul(mesh_latent, weights_full[3]).astype(BF16)
     decode_out[...] = silu(matmul_tn(decode_pick, mesh_project) + decode_attr).astype(BF16)
     send_all(*dec)
-    hand_on(5)
+    hand_over(5)
+    loaded("out", "target")
     ready(5)
     recv_all(*dec)
 
     collected[...] = matmul(decode_collect, decode_in[...]).astype(BF16)
     incoming = matmul(collected[...], weights_full[4])
     decoded = (latent[...].astype(F32) + incoming).astype(BF16)
-    predicted = matmul(decoded, out_weight[...]).astype(BF16)
+    predicted = matmul_nt(out_weight[...], decoded).astype(BF16)
     predicted_ref[...] = predicted
     scale = math.sqrt(grid_rows * nb * nf * 2)
     error = ((predicted.astype(F32) - target[...].astype(F32)) / scale).astype(BF16)
-    cotangent = matmul_nt(error, out_weight[...]).astype(BF16)
+    cotangent = matmul_tn(error, out_weight[...]).astype(BF16)
 
     if not inside:
         gradient_ref[...] = matmul_tn(collected[...], cotangent)
@@ -347,15 +445,18 @@
 
         for k in range(1, lane):
             final(k).start()
-        gradient_ref[rows_of(spot), :] = final_out[...].astype(F32)
+        gradient_ref[rows_of(spot), :] = final_out[...]
         for k in range(1, lane):
             final(k).wait_recv()
-            gradient_ref[rows_of(lax.rem(spot + lane - k, lane)), :] = final_in[k - 1].astype(F32)
+            gradient_ref[rows_of(lax.rem(spot + lane - k, lane)), :] = final_in[k - 1]
 
     for i in range(6):
         for off in range(1, nf):
             across(i, off).wait_send()
-            handed(i, off).wait_send()
+            for dy in range(npart):
+                handed(i, off, dy).wait_send()
+            for dy in range(1, npart):
+                traded(i, off, dy).wait_send()
     sent_all(*enc)
     sent_all(*dec)
     if inside:
@@ -367,39 +468,45 @@
 
 
 def local(sizes, *args):
-    nb, nf, inside = sizes
+    npart, nb, nf, inside = sizes
     args = list(args)
-    grid_in, mesh_in = args[0], args[2]
+    mesh_in = args[2]
+    for at in (0, 1, 12):
+        args[at] = args[at].T
+    values, grid_rows = args[0].shape
     width = mesh_in.shape[1]
     columns = width // nf
     args[8] = args[8].reshape(1, width)
-    for at in (13, 14, 16, 17):
-        args[at] = args[at].reshape(1, -1)
-    cap_e = args[13].shape[1]
-    cap_d = args[16].shape[1]
+    cap_e = math.prod(args[13].shape)
+    cap_d = math.prod(args[16].shape)
     half = width // 2
     rows = half // nb if inside else 16
-    padded = -(-grid_in.shape[1] // 32) * 32
+    padded = -(-values // (32 * npart)) * 32 * npart
     slots = max(nf - 1, 1)
+    trades = max(npart - 1, 1)
     dma = pltpu.SemaphoreType.DMA
     group, lane = (nb * nf, nb * 2) if inside else (2, 2)
+    held = (0, 1, 2, 3, 5, 8, 10, 12, 13, 14, 15, 16, 17, 18)
     predicted, gradient = pl.pallas_call(
         functools.partial(forecaster, sizes),
         out_shape=(
-            jax.ShapeDtypeStruct(grid_in.shape, BF16),
-            jax.ShapeDtypeStruct((width, columns if inside else width), F32),
+            jax.ShapeDtypeStruct((values, grid_rows), BF16),
+            jax.ShapeDtypeStruct(
+                (width, columns if inside else width), BF16 if inside else F32
+            ),
         ),
-        in_specs=[pl.BlockSpec(memory_space=pltpu.VMEM)] * len(args),
+        in_specs=[pl.BlockSpec(memory_space=pltpu.HBM)] * len(args),
         out_specs=(pl.BlockSpec(memory_space=pltpu.VMEM),) * 2,
-        scratch_shapes=[
+        scratch_shapes=[pltpu.VMEM(args[at].shape, args[at].dtype) for at in held]
+        + [
             pltpu.VMEM((padded, width), BF16),
             pltpu.VMEM((5, width, width), BF16),
-            pltpu.VMEM((grid_in.shape[0], width), BF16),
+            pltpu.VMEM((grid_rows, width), BF16),
             pltpu.VMEM((cap_e, width), BF16),
             pltpu.VMEM((cap_e, width), BF16),
             pltpu.VMEM((cap_d, width), BF16),
             pltpu.VMEM((cap_d, width), BF16),
-            pltpu.VMEM((grid_in.shape[0], width), BF16),
+            pltpu.VMEM((grid_rows, width), BF16),
             pltpu.VMEM((half, width), BF16),
             pltpu.VMEM((half, width), BF16),
             pltpu.VMEM((half, width), F32),
@@ -407,10 +514,14 @@
             pltpu.VMEM((group - 1, rows, columns), BF16),
             pltpu.VMEM((rows, columns), BF16),
             pltpu.VMEM((lane - 1, rows, columns), BF16),
+            dma((len(held),)),
+            dma((5,)),
             dma((6, slots)),
             dma((6, slots)),
-            dma((6, slots)),
-            dma((6, slots)),
+            dma((6, slots, trades)),
+            dma((6, slots, trades)),
+            dma((6, slots, npart)),
+            dma((6, slots, npart)),
             dma((len(HOPS),)),
             dma((len(HOPS),)),
             dma((len(HOPS),)),
@@ -425,18 +536,20 @@
             collective_id=0, has_side_effects=True, vmem_limit_bytes=48 * 1024 * 1024
         ),
     )(*args)
-    if not inside:
+    if inside:
+        gradient = gradient.astype(F32)
+    else:
         total = lax.psum(gradient, ("band", "feat", "rep"))
         gradient = lax.dynamic_slice_in_dim(total, lax.axis_index("feat") * columns, columns, 1)
-    return (predicted, gradient)
+    return (predicted.T, gradient)
 
 
 def solution(mesh):
-    nb, nf = mesh.shape["band"], mesh.shape["feat"]
+    npart, nb, nf = mesh.shape["parts"], mesh.shape["band"], mesh.shape["feat"]
     inside = nb <= 8 and nf <= 2
     slab = ("parts", "band", "feat", "rep")
     return jax.shard_map(
-        functools.partial(local, (nb, nf, inside)),
+        functools.partial(local, (npart, nb, nf, inside)),
         mesh=mesh,
         in_specs=(
             P(slab, None),

time: 53.7 us -> 65.3 us (1.22)
  local copies, waits for them, and re-layouts: 7.7 us -> 15 us
  Pallas kernels: 44.9 us -> 48.1 us
  other arithmetic: 0 us -> 0.83 us
    unnamed x38 -> x37, local copies, waits for them, and re-layouts: 5.83 us -> 14.3 us
    pallas_call x1, Pallas kernels: 44.9 us -> 48.1 us  [local(): pl.pallas_call(functools.partial(forecaster, sizes), out_shape=(jax.Shape...]
    reshape x4 -> x0, local copies, waits for them, and re-layouts: 1.02 us -> none  [local(): args[at] = args[at].reshape(1, -1)]
    pallas_call x1 -> x0, local copies, waits for them, and re-layouts: 0.85 us -> none  [local(): pl.pallas_call(functools.partial(forecaster, sizes), out_shape=(jax.Shape...]
    convert_element_type x0 -> x1, other arithmetic: none -> 0.83 us  [local(): gradient = gradient.astype(F32)]
    reshape x1, local copies, waits for them, and re-layouts: 0.01 us -> 0.69 us  [local(): args[8] = args[8].reshape(1, width)]
where the time goes in v2:
time: 65.3 us; the launch traced here: 64.6 us
  Pallas kernels  48.1 us (74%)
  local copies, waits for them, and re-layouts  15 us (23%)
  other arithmetic  0.83 us (1%)
  between operations  0.68 us (1%)
    pallas_call x1, Pallas kernels, local(): pl.pallas_call(functools.partial(forecaster, sizes), out_shape=(jax.Shape...  48.1 us
    unnamed x37, local copies, waits for them, and re-layouts  14.3 us

profile of v2, /device:TPU:0, one launch (start us, length us, event | category | flops | bytes accessed | tf_op | source)
XLA Modules:
  0.0 64.6 jit_solution(7979261415587115988)
XLA Ops:
  0.6 0.0 copy-start.11
  0.6 0.0 copy-start.10
  0.7 0.7 %reshape.7.node_gain_hbm = bf16[1,512]{1,0:T(2,128)(2,1)S(1)} reshape(bf16[512]{0:T(512)(128)(2,1)} %param.27) | data formatting | bytes 2048 | tf_op jit(solution)/shard_map/reshape | solution.py:479
  1.3 0.0 copy-done.11
  1.3 0.0 copy-done.10
  1.4 1.0 %copy-done = bf16[512,520]{0,1:T(8,128)(2,1)S(1)} copy-done((bf16[512,520]{0,1:T(8,128)(2,1)S(1)}, bf16[512,520]{0,1:T(8,128)(2,1)}, u32[]{:S(2)}) %copy-start) | copy-done | bytes 532504
  2.4 0.9 %copy-done.1 = bf16[256,520]{0,1:T(8,128)(2,1)S(1)} copy-done((bf16[256,520]{0,1:T(8,128)(2,1)S(1)}, bf16[256,520]{0,1:T(8,128)(2,1)}, u32[]{:S(2)}) %copy-start.1) | copy-done | bytes 266264
  3.4 0.9 %copy-done.2 = bf16[256,520]{0,1:T(8,128)(2,1)S(1)} copy-done((bf16[256,520]{0,1:T(8,128)(2,1)S(1)}, bf16[256,520]{0,1:T(8,128)(2,1)}, u32[]{:S(2)}) %copy-start.2) | copy-done | bytes 266264
  4.3 0.9 %copy-done.3 = bf16[520,256]{1,0:T(8,128)(2,1)S(1)} copy-done((bf16[520,256]{1,0:T(8,128)(2,1)S(1)}, bf16[520,256]{1,0:T(8,128)(2,1)}, u32[]{:S(2)}) %copy-start.3) | copy-done | bytes 266264
  5.3 0.9 %copy-done.4 = bf16[512,256]{1,0:T(8,128)(2,1)S(1)} copy-done((bf16[512,256]{1,0:T(8,128)(2,1)S(1)}, bf16[512,256]{1,0:T(8,128)(2,1)}, u32[]{:S(2)}) %copy-start.4) | copy-done | bytes 262168
  6.2 0.9 %copy-done.5 = bf16[512,256]{1,0:T(8,128)(2,1)S(1)} copy-done((bf16[512,256]{1,0:T(8,128)(2,1)S(1)}, bf16[512,256]{1,0:T(8,128)(2,1)}, u32[]{:S(2)}) %copy-start.5) | copy-done | bytes 262168
  7.2 0.9 %copy-done.6 = bf16[512,256]{1,0:T(8,128)(2,1)S(1)} copy-done((bf16[512,256]{1,0:T(8,128)(2,1)S(1)}, bf16[512,256]{1,0:T(8,128)(2,1)}, u32[]{:S(2)}) %copy-start.6) | copy-done | bytes 262168
  8.1 0.9 %copy-done.7 = bf16[512,256]{1,0:T(8,128)(2,1)S(1)} copy-done((bf16[512,256]{1,0:T(8,128)(2,1)S(1)}, bf16[512,256]{1,0:T(8,128)(2,1)}, u32[]{:S(2)}) %copy-start.7) | copy-done | bytes 262168
  9.1 0.9 %copy-done.8 = bf16[512,256]{1,0:T(8,128)(2,1)S(1)} copy-done((bf16[512,256]{1,0:T(8,128)(2,1)S(1)}, bf16[512,256]{1,0:T(8,128)(2,1)}, u32[]{:S(2)}) %copy-start.8) | copy-done | bytes 262168
  10.0 0.9 %copy-done.9 = bf16[128,512]{1,0:T(8,128)(2,1)S(1)} copy-done((bf16[128,512]{1,0:T(8,128)(2,1)S(1)}, bf16[128,512]{1,0:T(8,128)(2,1)}, u32[]{:S(2)}) %copy-start.9) | copy-done | bytes 131096
  10.9 0.7 %copy-done.12 = s32[1,4,32]{2,1,0:T(4,128)S(1)} copy-done((s32[1,4,32]{2,1,0:T(4,128)S(1)}, s32[1,4,32]{2,1,0:T(4,128)}, u32[]{:S(2)}) %copy-start.12) | copy-done | bytes 536
  11.6 0.7 %copy-done.13 = s32[1,4,32]{2,1,0:T(4,128)S(1)} copy-done((s32[1,4,32]{2,1,0:T(4,128)S(1)}, s32[1,4,32]{2,1,0:T(4,128)}, u32[]{:S(2)}) %copy-start.13) | copy-done | bytes 536
  12.3 0.7 %copy-done.14 = s32[1,4,64]{2,1,0:T(4,128)S(1)} copy-done((s32[1,4,64]{2,1,0:T(4,128)S(1)}, s32[1,4,64]{2,1,0:T(4,128)}, u32[]{:S(2)}) %copy-start.14) | copy-done | bytes 1048
  13.0 0.7 %copy-done.15 = s32[1,4,64]{2,1,0:T(4,128)S(1)} copy-done((s32[1,4,64]{2,1,0:T(4,128)S(1)}, s32[1,4,64]{2,1,0:T(4,128)}, u32[]{:S(2)}) %copy-start.15) | copy-done | bytes 1048
  13.6 0.7 %copy-done.16 = bf16[1,4,256]{2,1,0:T(4,128)(2,1)S(1)} copy-done((bf16[1,4,256]{2,1,0:T(4,128)(2,1)S(1)}, bf16[1,4,256]{2,1,0:T(4,128)(2,1)}, u32[]{:S(2)}) %copy-start.16) | copy-done | bytes 2072
  14.3 0.7 %copy-done.17 = bf16[1,4,128]{2,1,0:T(4,128)(2,1)S(1)} copy-done((bf16[1,4,128]{2,1,0:T(4,128)(2,1)S(1)}, bf16[1,4,128]{2,1,0:T(4,128)(2,1)}, u32[]{:S(2)}) %copy-start.17) | copy-done | bytes 1048
  15.0 48.1 %shard_map.194 = (bf16[520,256]{1,0:T(8,128)(2,1)S(1)}, bf16[512,256]{1,0:T(8,128)(2,1)S(1)}) custom-call(bf16[520,256]{1,0:T(8,128)(2,1)S(1)} %bitcast.5, bf16[520,256]{1,0:T(8,128)(2,1)S(1)} %bitcast.6, bf16[128,512]{1,0:T(8,128)(2,1)S(1)} %copy-done.9, bf16[520,256]{1,0:T(8,128)(2,1)S(1)} %copy-done.3, bf16[512,256]{1,0:T(8,128)(2,1)S(1)} %copy-done.4, ...), custom_call_target="tpu_custom_call" | custom-call | tf_op jit(solution)/shard_map/pallas_call | solution.py:490
  63.1 0.8 %convert_element_type.3 = f32[512,256]{1,0:T(8,128)} convert(bf16[512,256]{1,0:T(8,128)(2,1)S(1)} %get-tuple-element.5) | non-fusion elementwise | flops 131072 | bytes 786432 | tf_op jit(solution)/shard_map/convert_element_type | solution.py:540
  63.9 0.7 %copy.22 = bf16[256,520]{0,1:T(8,128)(2,1)} copy(bf16[256,520]{0,1:T(8,128)(2,1)S(1)} %bitcast.7) | data formatting | bytes 532480
  (16 shorter events, 0.0 us)
Async XLA Ops:
  0.6 0.7 %copy-start.11 = (bf16[4,512]{1,0:T(4,128)(2,1)S(1)}, bf16[4,512]{1,0:T(4,128)(2,1)}, u32[]{:S(2)}) copy-start(bf16[4,512]{1,0:T(4,128)(2,1)} %decode_attr_hbm.1) | copy-start | bytes 12292
  0.6 0.7 %copy-start.10 = (bf16[4,512]{1,0:T(4,128)(2,1)S(1)}, bf16[4,512]{1,0:T(4,128)(2,1)}, u32[]{:S(2)}) copy-start(bf16[4,512]{1,0:T(4,128)(2,1)} %encode_attr_hbm.1) | copy-start | bytes 12292
  1.4 1.0 %copy-start = (bf16[512,520]{0,1:T(8,128)(2,1)S(1)}, bf16[512,520]{0,1:T(8,128)(2,1)}, u32[]{:S(2)}) copy-start(bf16[512,520]{0,1:T(8,128)(2,1)} %param.31) | copy-start | bytes 1597444
  2.4 1.0 %copy-start.1 = (bf16[256,520]{0,1:T(8,128)(2,1)S(1)}, bf16[256,520]{0,1:T(8,128)(2,1)}, u32[]{:S(2)}) copy-start(bf16[256,520]{0,1:T(8,128)(2,1)} %param.19) | copy-start | bytes 798724
  3.3 1.0 %copy-start.2 = (bf16[256,520]{0,1:T(8,128)(2,1)S(1)}, bf16[256,520]{0,1:T(8,128)(2,1)}, u32[]{:S(2)}) copy-start(bf16[256,520]{0,1:T(8,128)(2,1)} %param.20) | copy-start | bytes 798724
  4.3 1.0 %copy-start.3 = (bf16[520,256]{1,0:T(8,128)(2,1)S(1)}, bf16[520,256]{1,0:T(8,128)(2,1)}, u32[]{:S(2)}) copy-start(bf16[520,256]{1,0:T(8,128)(2,1)} %embed_hbm.1) | copy-start | bytes 798724
  5.3 0.9 %copy-start.4 = (bf16[512,256]{1,0:T(8,128)(2,1)S(1)}, bf16[512,256]{1,0:T(8,128)(2,1)}, u32[]{:S(2)}) copy-start(bf16[512,256]{1,0:T(8,128)(2,1)} %encode_project_hbm.1) | copy-start | bytes 786436
  6.2 0.9 %copy-start.5 = (bf16[512,256]{1,0:T(8,128)(2,1)S(1)}, bf16[512,256]{1,0:T(8,128)(2,1)}, u32[]{:S(2)}) copy-start(bf16[512,256]{1,0:T(8,128)(2,1)} %encode_edge_hbm.1) | copy-start | bytes 786436
  7.2 0.9 %copy-start.6 = (bf16[512,256]{1,0:T(8,128)(2,1)S(1)}, bf16[512,256]{1,0:T(8,128)(2,1)}, u32[]{:S(2)}) copy-start(bf16[512,256]{1,0:T(8,128)(2,1)} %node_weight_hbm.1) | copy-start | bytes 786436
  8.1 0.9 %copy-start.7 = (bf16[512,256]{1,0:T(8,128)(2,1)S(1)}, bf16[512,256]{1,0:T(8,128)(2,1)}, u32[]{:S(2)}) copy-start(bf16[512,256]{1,0:T(8,128)(2,1)} %decode_project_hbm.1) | copy-start | bytes 786436
  9.1 0.9 %copy-start.8 = (bf16[512,256]{1,0:T(8,128)(2,1)S(1)}, bf16[512,256]{1,0:T(8,128)(2,1)}, u32[]{:S(2)}) copy-start(bf16[512,256]{1,0:T(8,128)(2,1)} %decode_edge_hbm.1) | copy-start | bytes 786436
  10.0 0.9 %copy-start.9 = (bf16[128,512]{1,0:T(8,128)(2,1)S(1)}, bf16[128,512]{1,0:T(8,128)(2,1)}, u32[]{:S(2)}) copy-start(bf16[128,512]{1,0:T(8,128)(2,1)} %mesh_in_hbm.1) | copy-start | bytes 393220
  10.9 0.7 %copy-start.12 = (s32[1,4,32]{2,1,0:T(4,128)S(1)}, s32[1,4,32]{2,1,0:T(4,128)}, u32[]{:S(2)}) copy-start(s32[1,4,32]{2,1,0:T(4,128)} %encode_senders_hbm.1) | copy-start | bytes 1540
  11.6 0.7 %copy-start.13 = (s32[1,4,32]{2,1,0:T(4,128)S(1)}, s32[1,4,32]{2,1,0:T(4,128)}, u32[]{:S(2)}) copy-start(s32[1,4,32]{2,1,0:T(4,128)} %encode_receivers_hbm.1) | copy-start | bytes 1540
  12.3 0.7 %copy-start.14 = (s32[1,4,64]{2,1,0:T(4,128)S(1)}, s32[1,4,64]{2,1,0:T(4,128)}, u32[]{:S(2)}) copy-start(s32[1,4,64]{2,1,0:T(4,128)} %decode_senders_hbm.1) | copy-start | bytes 3076
  13.0 0.7 %copy-start.15 = (s32[1,4,64]{2,1,0:T(4,128)S(1)}, s32[1,4,64]{2,1,0:T(4,128)}, u32[]{:S(2)}) copy-start(s32[1,4,64]{2,1,0:T(4,128)} %decode_receivers_hbm.1) | copy-start | bytes 3076
  13.6 0.7 %copy-start.16 = (bf16[1,4,256]{2,1,0:T(4,128)(2,1)S(1)}, bf16[1,4,256]{2,1,0:T(4,128)(2,1)}, u32[]{:S(2)}) copy-start(bf16[1,4,256]{2,1,0:T(4,128)(2,1)} %decode_features_hbm.1) | copy-start | bytes 6148
  14.3 0.7 %copy-start.17 = (bf16[1,4,128]{2,1,0:T(4,128)(2,1)S(1)}, bf16[1,4,128]{2,1,0:T(4,128)(2,1)}, u32[]{:S(2)}) copy-start(bf16[1,4,128]{2,1,0:T(4,128)(2,1)} %encode_features_hbm.1) | copy-start | bytes 3076

commit v3 on v2

--- a/solution.py
+++ b/solution.py
@@ -109,14 +109,13 @@
 ):
     npart, nb, nf, inside = sizes
     band, feat, rep = lax.axis_index("band"), lax.axis_index("feat"), lax.axis_index("rep")
-    side = lax.axis_index("parts")
+    side = lax.axis_index("parts") if npart > 1 else 0
     other = 1 - rep
     width = mesh_in.shape[1]
     columns = width // nf
     values, grid_rows = grid_in.shape
     mesh_rows = mesh_in.shape[0]
     group = nb * nf
-    lane = nb * 2
     shares = npart * 2
 
     def in_range(b):
@@ -129,17 +128,11 @@
     for dy in range(1, npart):
         greet({"parts": lax.rem(side + dy, npart)})
     if inside:
+        greet({"rep": other})
         for db in range(nb):
             for df in range(nf):
-                for dr in range(2):
-                    if (db or df or dr) and not (df and dr):
-                        greet(
-                            {
-                                "band": lax.rem(band + db, nb),
-                                "feat": lax.rem(feat + df, nf),
-                                "rep": lax.rem(rep + dr, 2),
-                            }
-                        )
+                if db or df:
+                    greet({"band": lax.rem(band + db, nb), "feat": lax.rem(feat + df, nf)})
     else:
         greet({"rep": other})
         for df in range(1, nf):
@@ -176,7 +169,7 @@
             loads[name].wait()
 
     own = pl.ds(pl.multiple_of(feat * columns, columns), columns)
-    padded = embed_full.shape[0]
+    padded = embed_full.shape[1]
     shards = (
         encode_project_hbm,
         encode_edge_hbm,
@@ -186,7 +179,7 @@
     )
     owns = []
     for i, shard in enumerate(shards):
-        owns.append(pltpu.make_async_copy(shard, weights_full.at[i, :, own], own_sem.at[i]))
+        owns.append(pltpu.make_async_copy(shard, weights_full.at[i, feat], own_sem.at[i]))
         owns[i].start()
     cap_e = encode_out.shape[0] // nb
     cap_d = decode_out.shape[0] // nb
@@ -196,12 +189,12 @@
             encode_in[pl.ds(p * cap_e, cap_e), :] = jnp.zeros((cap_e, width), BF16)
             decode_in[pl.ds(p * cap_d, cap_d), :] = jnp.zeros((cap_d, width), BF16)
     base = values // 32 * 32
-    embed_full[pl.ds(base, padded - base), own] = jnp.zeros((padded - base, columns), BF16)
+    embed_full[feat, pl.ds(base, padded - base), :] = jnp.zeros((padded - base, columns), BF16)
     loaded("embed")
-    embed_full[pl.ds(0, values), own] = embed_own[...]
+    embed_full[feat, pl.ds(0, values), :] = embed_own[...]
 
     if inside:
-        pl.semaphore_wait(barrier, npart - 1 + nb * (nf + 1) - 1)
+        pl.semaphore_wait(barrier, npart - 1 + group)
     else:
         pl.semaphore_wait(barrier, npart - 1 + nf)
         for d in HOPS:
@@ -217,10 +210,9 @@
         return pl.ds(pl.multiple_of((y * 2 + r) * h, 16), h)
 
     def part(i, y, r, f):
-        cols = pl.ds(pl.multiple_of(f * columns, columns), columns)
         if i == 0:
-            return embed_full.at[spot_of(i, y, r), cols]
-        return weights_full.at[i - 1, spot_of(i, y, r), cols]
+            return embed_full.at[f, spot_of(i, y, r), :]
+        return weights_full.at[i - 1, f, spot_of(i, y, r), :]
 
     def across(i, off):
         view = part(i, side, rep, feat)
@@ -319,6 +311,9 @@
     enc = (encode_out, encode_in, e_send, e_recv, cap_e)
     dec = (decode_out, decode_in, d_send, d_recv, cap_d)
 
+    def weigh(activation, i):
+        return jnp.concatenate([matmul(activation, weights_full[i, f]) for f in range(nf)], axis=1)
+
     def slot_row(blocks):
         return jnp.concatenate([blocks[0, pl.ds(p, 1), :] for p in range(nb)], axis=1)
 
@@ -329,11 +324,15 @@
     hand_on(1)
     hand_over(0)
     ready(0)
-    latent[...] = silu(matmul_tn(grid_in[...], embed_full[pl.ds(0, values), :])).astype(BF16)
+    latent[...] = silu(
+        jnp.concatenate(
+            [matmul_tn(grid_in[...], embed_full[f, pl.ds(0, values), :]) for f in range(nf)], axis=1
+        )
+    ).astype(BF16)
     hand_over(1)
     hand_on(2)
     ready(1)
-    grid_project = matmul(latent[...], weights_full[0]).astype(BF16)
+    grid_project = weigh(latent[...], 0).astype(BF16)
     encode_out[...] = silu(matmul_tn(encode_pick, grid_project) + encode_attr).astype(BF16)
     send_all(*enc)
 
@@ -349,17 +348,17 @@
     recv_all(*enc)
     gathered = matmul(encode_collect, encode_in[...]).astype(BF16)
     ready(2)
-    aggregated = matmul(gathered, weights_full[1]).astype(BF16)
+    aggregated = weigh(gathered, 1).astype(BF16)
     loaded("mesh", "gain")
     ready(3)
-    update = mesh_in[...].astype(F32) + matmul(aggregated, weights_full[2])
+    update = mesh_in[...].astype(F32) + weigh(aggregated, 2)
     hand_over(4)
     hand_on(5)
     centered = update - jnp.mean(update, axis=-1, keepdims=True)
     spread = jnp.mean(centered * centered, axis=-1, keepdims=True)
-    mesh_latent = (node_gain[...].astype(F32) * centered * lax.rsqrt(spread + eps_norm)).astype(BF16)
+    mesh_latent = (node_gain[...].astype(F32).reshape(1, width) * centered * lax.rsqrt(spread + eps_norm)).astype(BF16)
     ready(4)
-    mesh_project = matmul(mesh_latent, weights_full[3]).astype(BF16)
+    mesh_project = weigh(mesh_latent, 3).astype(BF16)
     decode_out[...] = silu(matmul_tn(decode_pick, mesh_project) + decode_attr).astype(BF16)
     send_all(*dec)
     hand_over(5)
@@ -368,7 +367,7 @@
     recv_all(*dec)
 
     collected[...] = matmul(decode_collect, decode_in[...]).astype(BF16)
-    incoming = matmul(collected[...], weights_full[4])
+    incoming = weigh(collected[...], 4)
     decoded = (latent[...].astype(F32) + incoming).astype(BF16)
     predicted = matmul_nt(out_weight[...], decoded).astype(BF16)
     predicted_ref[...] = predicted
@@ -426,29 +425,42 @@
             piece(k).wait_recv()
             total = total + pieces_in[k - 1].astype(F32)
         final_out[...] = total.astype(BF16)
-        spot = band * 2 + rep
-
-        def final(k):
-            to = lax.rem(spot + k, lane)
+
+        def around(k):
             return pltpu.make_async_remote_copy(
                 src_ref=final_out,
                 dst_ref=final_in.at[k - 1],
                 send_sem=g_send.at[k - 1],
                 recv_sem=g_recv.at[k - 1],
-                device_id={"band": lax.div(to, 2), "rep": lax.rem(to, 2)},
+                device_id={"band": lax.rem(band + k, nb)},
                 device_id_type=MESH,
             )
 
-        def rows_of(s):
-            start = lax.rem(s, 2) * half + lax.div(s, 2) * rows
+        def beside(k):
+            return pltpu.make_async_remote_copy(
+                src_ref=final_in.at[k - 1] if k else final_out,
+                dst_ref=final_in.at[nb - 1 + k],
+                send_sem=g_send.at[nb - 1 + k],
+                recv_sem=g_recv.at[nb - 1 + k],
+                device_id={"rep": other},
+                device_id_type=MESH,
+            )
+
+        def rows_of(r, k):
+            start = r * half + lax.rem(band + nb - k, nb) * rows
             return pl.ds(pl.multiple_of(start, 16), rows)
 
-        for k in range(1, lane):
-            final(k).start()
-        gradient_ref[rows_of(spot), :] = final_out[...]
-        for k in range(1, lane):
-            final(k).wait_recv()
-            gradient_ref[rows_of(lax.rem(spot + lane - k, lane)), :] = final_in[k - 1]
+        for k in range(1, nb):
+            around(k).start()
+        beside(0).start()
+        gradient_ref[rows_of(rep, 0), :] = final_out[...].astype(F32)
+        for k in range(1, nb):
+            around(k).wait_recv()
+            beside(k).start()
+            gradient_ref[rows_of(rep, k), :] = final_in[k - 1].astype(F32)
+        for k in range(nb):
+            beside(k).wait_recv()
+            gradient_ref[rows_of(other, k), :] = final_in[nb - 1 + k].astype(F32)
 
     for i in range(6):
         for off in range(1, nf):
@@ -463,8 +475,10 @@
         swap.wait_send()
         for k in range(1, group):
             piece(k).wait_send()
-        for k in range(1, lane):
-            final(k).wait_send()
+        for k in range(1, nb):
+            around(k).wait_send()
+        for k in range(nb):
+            beside(k).wait_send()
 
 
 def local(sizes, *args):
@@ -476,7 +490,6 @@
     values, grid_rows = args[0].shape
     width = mesh_in.shape[1]
     columns = width // nf
-    args[8] = args[8].reshape(1, width)
     cap_e = math.prod(args[13].shape)
     cap_d = math.prod(args[16].shape)
     half = width // 2
@@ -491,16 +504,14 @@
         functools.partial(forecaster, sizes),
         out_shape=(
             jax.ShapeDtypeStruct((values, grid_rows), BF16),
-            jax.ShapeDtypeStruct(
-                (width, columns if inside else width), BF16 if inside else F32
-            ),
+            jax.ShapeDtypeStruct((width, columns if inside else width), F32),
         ),
-        in_specs=[pl.BlockSpec(memory_space=pltpu.HBM)] * len(args),
+        in_specs=[pl.BlockSpec(memory_space=pl.ANY)] * len(args),
         out_specs=(pl.BlockSpec(memory_space=pltpu.VMEM),) * 2,
         scratch_shapes=[pltpu.VMEM(args[at].shape, args[at].dtype) for at in held]
         + [
-            pltpu.VMEM((padded, width), BF16),
-            pltpu.VMEM((5, width, width), BF16),
+            pltpu.VMEM((nf, padded, columns), BF16),
+            pltpu.VMEM((5, nf, width, columns), BF16),
             pltpu.VMEM((grid_rows, width), BF16),
             pltpu.VMEM((cap_e, width), BF16),
             pltpu.VMEM((cap_e, width), BF16),
@@ -533,19 +544,17 @@
             dma((lane - 1,)),
         ],
         compiler_params=pltpu.CompilerParams(
-            collective_id=0, has_side_effects=True, vmem_limit_bytes=48 * 1024 * 1024
+            collective_id=0, has_side_effects=True, vmem_limit_bytes=63 * 1024 * 1024
         ),
     )(*args)
-    if inside:
-        gradient = gradient.astype(F32)
-    else:
+    if not inside:
         total = lax.psum(gradient, ("band", "feat", "rep"))
         gradient = lax.dynamic_slice_in_dim(total, lax.axis_index("feat") * columns, columns, 1)
     return (predicted.T, gradient)
 
 
 def solution(mesh):
-    npart, nb, nf = mesh.shape["parts"], mesh.shape["band"], mesh.shape["feat"]
+    npart, nb, nf = 1, mesh.shape["band"], mesh.shape["feat"]
     inside = nb <= 8 and nf <= 2
     slab = ("parts", "band", "feat", "rep")
     return jax.shard_map(

time: 65.3 us -> 50.3 us (0.77)
  local copies, waits for them, and re-layouts: 15 us -> 2.53 us
  Pallas kernels: 48.1 us -> 47 us
  other arithmetic: 0.83 us -> 0 us
    unnamed x37 -> x4, local copies, waits for them, and re-layouts: 14.3 us -> 2.53 us
    pallas_call x1, Pallas kernels: 48.1 us -> 47 us  [local(): pl.pallas_call(functools.partial(forecaster, sizes), out_shape=(jax.Shape...]
    convert_element_type x1 -> x0, other arithmetic: 0.83 us -> none  [local(): gradient = gradient.astype(F32)]
    reshape x1 -> x0, local copies, waits for them, and re-layouts: 0.69 us -> none  [local(): args[8] = args[8].reshape(1, width)]
where the time goes in v3:
time: 50.3 us; the launch traced here: 50.2 us
  Pallas kernels  47 us (93%)
  local copies, waits for them, and re-layouts  2.53 us (5%)
  between operations  0.66 us (1%)
    pallas_call x1, Pallas kernels, local(): pl.pallas_call(functools.partial(forecaster, sizes), out_shape=(jax.Shape...  47 us
    unnamed x4, local copies, waits for them, and re-layouts  2.53 us

profile of v3, /device:TPU:0, one launch (start us, length us, event | category | flops | bytes accessed | tf_op | source)
XLA Modules:
  0.0 50.2 jit_solution(3201144422505326480)
XLA Ops:
  0.6 47.0 %shard_map.194 = (bf16[520,256]{1,0:T(8,128)(2,1)}, f32[512,256]{1,0:T(8,128)}) custom-call(bf16[520,256]{1,0:T(8,128)(2,1)} %bitcast.6, bf16[520,256]{1,0:T(8,128)(2,1)} %bitcast.7, bf16[128,512]{1,0:T(8,128)(2,1)} %mesh_in_hbm.1, bf16[520,256]{1,0:T(8,128)(2,1)} %embed_hbm.1, bf16[512,256]{1,0:T(8,128)(2,1)} %encode_project_hbm.1, ...), custom_call_target="tpu_custom_call" | custom-call | tf_op jit(solution)/shard_map/pallas_call | solution.py:503
  47.6 0.0 copy-start
  47.6 1.7 %copy.23 = bf16[256,520]{0,1:T(8,128)(2,1)} copy(bf16[256,520]{0,1:T(8,128)(2,1)} %bitcast.5) | data formatting | bytes 532480
  49.4 0.0 copy-done
  49.4 0.8 %copy.24 = f32[512,256]{1,0:T(8,128)} copy(f32[512,256]{1,0:T(8,128)S(1)} %copy-done) | data formatting | bytes 1048576
Async XLA Ops:
  47.6 1.7 %copy-start = (f32[512,256]{1,0:T(8,128)S(1)}, f32[512,256]{1,0:T(8,128)}, u32[]{:S(2)}) copy-start(f32[512,256]{1,0:T(8,128)} %get-tuple-element.9) | copy-start | bytes 1572868
